TPU v7x, 256 devices: a whole 4x4x8 slice. The times are simulated.
256 devices in a mesh: row: 16 (over z_lo, y, core), col: 16 (over z_hi, x).
Axes of the slice: x: 4, y: 4, z: 8 (z_hi: 4, z_lo: 2; z = z_hi * 2 + z_lo), core: 2. Of those that a mesh axis runs over, the one named last changes fastest.
Arguments:
- source_desc: bfloat16 [32768, 64], P('row', 'col'), may hold values from -9 to 9
- target_desc: bfloat16 [32768, 64], P('col'), may hold values from -9 to 9
- source_mass: bfloat16 [32768], P('row'), may hold values from 0.099609375 to 10
- target_mass: bfloat16 [32768], P('col'), may hold values from 0.099609375 to 10
Outputs:
- cross_source: float32 [32768], P('row')
- cross_target: float32 [32768], P('col')
- self_source: float32 [32768], P('row')
- self_target: float32 [32768], P('col')
All inputs are finite; a program needn't handle non-finite values.
Results may differ from a plain program's by a relative error of at most 0.0003.
Values may be sent and summed in bfloat16 or wider, within the bound.
A program may use at most 64 MiB of HBM per device.

v0:
```python
import math
import jax
import jax.numpy as jnp
from jax import lax
from jax.sharding import PartitionSpec as P

ITERS = 2
EPSILON = 0.25
REACH = 1.0
DAMPING = 1.0 / (1.0 + EPSILON / REACH)


def half_norms(points):
    wide = points.astype(jnp.float32)
    return 0.5 * jnp.sum(wide * wide, axis=1)


def tile_stats(
    left_desc, right_desc, left_norm, right_norm, left_weight, right_weight, want_rows, want_cols
):
    count = left_desc.shape[0]
    block = math.gcd(512, count)
    blocks = count // block
    width = left_desc.shape[1]
    right_count = right_desc.shape[0]
    inputs = (
        left_desc.reshape(blocks, block, width),
        left_norm.reshape(blocks, block),
        left_weight.reshape(blocks, block),
    )

    def advance(carry, pieces):
        piece_desc, piece_norm, piece_weight = pieces
        product = lax.dot_general(
            piece_desc, right_desc, (((1,), (1,)), ((), ())), preferred_element_type=jnp.float32
        )
        scaled = (piece_norm[:, None] + right_norm[None, :] - product) / EPSILON
        emitted = ()
        if want_rows:
            row_score = right_weight[None, :] - scaled
            row_top = jnp.max(row_score, axis=1)
            row_total = jnp.sum(jnp.exp(row_score - row_top[:, None]), axis=1)
            emitted = (row_top, row_total)
        if want_cols:
            col_top, col_total = carry
            col_score = piece_weight[:, None] - scaled
            fresh_top = jnp.maximum(col_top, jnp.max(col_score, axis=0))
            col_total = col_total * jnp.exp(col_top - fresh_top) + jnp.sum(
                jnp.exp(col_score - fresh_top[None, :]), axis=0
            )
            carry = (fresh_top, col_total)
        return (carry, emitted)

    if want_cols:
        start = (
            jnp.full((right_count,), -jnp.inf, jnp.float32),
            jnp.zeros((right_count,), jnp.float32),
        )
    else:
        start = ()
    carry, emitted = lax.scan(advance, start, inputs)
    rows_out = (emitted[0].reshape(count), emitted[1].reshape(count)) if want_rows else None
    cols_out = carry if want_cols else None
    return (rows_out, cols_out)


def reduce_col(maxima, totals):
    merged_top = lax.pmax(maxima, "col")
    merged_total = lax.psum(totals * jnp.exp(maxima - merged_top), "col")
    return merged_top + jnp.log(merged_total)


def reduce_row(maxima, totals):
    merged_top = lax.pmax(maxima, "row")
    merged_total = lax.psum(totals * jnp.exp(maxima - merged_top), "row")
    return merged_top + jnp.log(merged_total)


def body(source_desc, target_desc, source_mass, target_mass):
    row_devices = lax.axis_size("row")
    col_devices = lax.axis_size("col")
    row_index = lax.axis_index("row")
    col_index = lax.axis_index("col")
    tile_count = source_mass.shape[0]
    source_part = tile_count // col_devices
    target_part = target_desc.shape[0] // row_devices
    mass_piece = lax.dynamic_slice_in_dim(source_mass, col_index * source_part, source_part, 0)
    source_rows = lax.all_gather(source_desc, "col", axis=1, tiled=True)
    desc_piece = lax.dynamic_slice_in_dim(source_rows, col_index * source_part, source_part, 0)
    source_cols, source_col_mass = (
        lax.all_gather(desc_piece, "row", axis=0, tiled=True),
        lax.all_gather(mass_piece, "row", axis=0, tiled=True),
    )
    target_piece = lax.dynamic_slice_in_dim(target_desc, row_index * target_part, target_part, 0)
    target_mass_piece = lax.dynamic_slice_in_dim(
        target_mass, row_index * target_part, target_part, 0
    )
    target_rows, target_row_mass = (
        lax.all_gather(target_piece, "col", axis=0, tiled=True),
        lax.all_gather(target_mass_piece, "col", axis=0, tiled=True),
    )
    source_log = jnp.log(source_mass.astype(jnp.float32))
    source_col_log = jnp.log(source_col_mass.astype(jnp.float32))
    target_log = jnp.log(target_mass.astype(jnp.float32))
    target_row_log = jnp.log(target_row_mass.astype(jnp.float32))
    source_row_norm = half_norms(source_rows)
    source_col_norm = half_norms(source_cols)
    target_col_norm = half_norms(target_desc)
    target_row_norm = half_norms(target_rows)
    cross_source = jnp.zeros((tile_count,), jnp.float32)
    cross_target = jnp.zeros((target_desc.shape[0],), jnp.float32)
    self_source = jnp.zeros((tile_count,), jnp.float32)
    self_target = jnp.zeros((target_desc.shape[0],), jnp.float32)
    source_view = jnp.zeros((source_cols.shape[0],), jnp.float32)
    target_view = jnp.zeros((target_rows.shape[0],), jnp.float32)
    for iteration in range(ITERS):
        mirror_work = iteration + 1 < ITERS
        cross_rows, cross_cols = tile_stats(
            source_rows,
            target_desc,
            source_row_norm,
            target_col_norm,
            source_log + cross_source / EPSILON,
            target_log + cross_target / EPSILON,
            True,
            True,
        )
        source_self_rows, source_self_cols = tile_stats(
            source_rows,
            source_cols,
            source_row_norm,
            source_col_norm,
            source_log + self_source / EPSILON,
            source_col_log + source_view / EPSILON,
            True,
            mirror_work,
        )
        target_self_rows, target_self_cols = tile_stats(
            target_rows,
            target_desc,
            target_row_norm,
            target_col_norm,
            target_row_log + target_view / EPSILON,
            target_log + self_target / EPSILON,
            mirror_work,
            True,
        )
        col_maxima = [cross_rows[0], source_self_rows[0]]
        col_totals = [cross_rows[1], source_self_rows[1]]
        row_maxima = [cross_cols[0], target_self_cols[0]]
        row_totals = [cross_cols[1], target_self_cols[1]]
        if mirror_work:
            col_maxima.append(target_self_rows[0])
            col_totals.append(target_self_rows[1])
            row_maxima.append(source_self_cols[0])
            row_totals.append(source_self_cols[1])
        col_logs = reduce_col(jnp.concatenate(col_maxima), jnp.concatenate(col_totals))
        row_logs = reduce_row(jnp.concatenate(row_maxima), jnp.concatenate(row_totals))
        target_count = target_desc.shape[0]
        cross_source = 0.5 * cross_source + 0.5 * DAMPING * (-EPSILON * col_logs[:tile_count])
        self_source = 0.5 * self_source + 0.5 * DAMPING * (
            -EPSILON * col_logs[tile_count : 2 * tile_count]
        )
        cross_target = 0.5 * cross_target + 0.5 * DAMPING * (-EPSILON * row_logs[:target_count])
        self_target = 0.5 * self_target + 0.5 * DAMPING * (
            -EPSILON * row_logs[target_count : 2 * target_count]
        )
        if mirror_work:
            target_view = 0.5 * target_view + 0.5 * DAMPING * (
                -EPSILON * col_logs[2 * tile_count :]
            )
            source_view = 0.5 * source_view + 0.5 * DAMPING * (
                -EPSILON * row_logs[2 * target_count :]
            )
    return (cross_source, cross_target, self_source, self_target)


def solution(mesh):
    return jax.shard_map(
        body,
        mesh=mesh,
        in_specs=(P("row", "col"), P("col", None), P("row"), P("col")),
        out_specs=(P("row"), P("col"), P("row"), P("col")),
        check_vma=False,
    )
```

profile of v0, /device:TPU:32, one launch (start us, length us, event | category | flops | bytes accessed | tf_op | source)
XLA Modules:
  0.0 824.4 jit_solution(18188859646712844108)
XLA Ops:
  0.6 47.2 %all-gather = bf16[16,4,2048]{2,1,0:T(4,128)(2,1)S(1)} all-gather(bf16[1,4,2048]{2,1,0:T(4,128)(2,1)} %bitcast.208), channel_id=1, replica_groups=mesh['row'=16,'col'=16] {'col'}, dimensions={0}, use_global_device_ids=true | all-gather | bytes 278528 | tf_op jit(solution)/shard_map/all_gather | solution.py:88
  47.9 20.2 %all_gather.16 = bf16[2048,64]{0,1:T(8,128)(2,1)S(1)} all-gather(bf16[128,64]{0,1:T(8,128)(2,1)S(1)} %dynamic-slice_bitcast_fusion), channel_id=1, replica_groups=mesh['row'=16,'col'=16] {'row'}, dimensions={0}, use_global_device_ids=true | all-gather | bytes 278528 | tf_op jit(solution)/shard_map/all_gather | solution.py:91
  69.3 16.1 %all-gather.1 = bf16[16,1,128]{2,1,0:T(2,128)(2,1)S(1)} all-gather(bf16[1,1,128]{2,1,0:T(2,128)(2,1)S(1)} %dynamic-slice_bitcast_fusion.2), channel_id=1, replica_groups=mesh['row'=16,'col'=16] {'row'}, dimensions={0}, use_global_device_ids=true | all-gather | bytes 4352 | tf_op jit(solution)/shard_map/all_gather | solution.py:92
  86.6 26.9 %while.95 = (s32[]{:T(128)}, f32[2048]{0:T(1024)S(1)}, f32[2048]{0:T(1024)S(1)}, f32[4,512]{1,0:T(4,128)S(1)}, f32[4,512]{1,0:T(4,128)S(1)}, /*index=5*/f32[4,51...) while((s32[]{:T(128)}, f32[2048]{0:T(1024)S(1)}, ...), condition=%wide.region_14.15_spmd.clone, body=%wide.region_9.14_spmd.clone.sunk | while | flops 147858432 | bytes 9203864 | solution.py:61
  89.8 3.4 exponential_reduce_fusion.18
  96.5 3.4 exponential_reduce_fusion.18
  103.3 3.4 exponential_reduce_fusion.18
  110.0 3.4 exponential_reduce_fusion.18
  113.7 26.7 %while.94 = (s32[]{:T(128)}, f32[2048]{0:T(1024)S(1)}, f32[2048]{0:T(1024)S(1)}, f32[4,512]{1,0:T(4,128)S(1)}, f32[4,512]{1,0:T(4,128)S(1)}, /*index=5*/f32[4,51...) while((s32[]{:T(128)}, f32[2048]{0:T(1024)S(1)}, ...), condition=%wide.region_7.8_spmd.clone, body=%wide.region_2.7_spmd.clone.sunk | while | flops 147858432 | bytes 8941720 | solution.py:61
  136.9 3.4 exponential_reduce_fusion.17
  140.5 39.3 %all_gather.19 = bf16[2048,64]{0,1:T(8,128)(2,1)S(1)} all-gather(bf16[128,64]{0,1:T(8,128)(2,1)S(1)} %constant_dynamic-slice_fusion.11), channel_id=1, replica_groups=mesh['row'=16,'col'=16] {'col'}, dimensions={0}, use_global_device_ids=true | all-gather | bytes 278528 | tf_op jit(solution)/shard_map/all_gather | solution.py:99
  180.3 39.8 %all-gather.2 = bf16[16,1,128]{2,1,0:T(2,128)(2,1)S(1)} all-gather(bf16[1,1,128]{2,1,0:T(2,128)(2,1)S(1)} %dynamic-slice_bitcast_fusion.1), channel_id=1, replica_groups=mesh['row'=16,'col'=16] {'col'}, dimensions={0}, use_global_device_ids=true | all-gather | bytes 4352 | tf_op jit(solution)/shard_map/all_gather | solution.py:100
  220.2 26.7 %while.96 = (s32[]{:T(128)}, f32[2048]{0:T(1024)S(1)}, f32[2048]{0:T(1024)S(1)}, f32[4,512]{1,0:T(4,128)S(1)}, f32[4,512]{1,0:T(4,128)S(1)}, /*index=5*/f32[4,51...) while((s32[]{:T(128)}, f32[2048]{0:T(1024)S(1)}, ...), condition=%wide.region_21.22_spmd.clone, body=%wide.region_16.21_spmd.clone.sunk | while | flops 147858432 | bytes 8941720 | solution.py:61
  246.9 76.7 %pmax.28 = f32[6144]{0:T(1024)S(1)} all-reduce(f32[6144]{0:T(1024)S(1)} %constant_dynamic-update-slice_fusion.8), channel_id=1, replica_groups=mesh['row'=16,'col'=16] {'col'}, use_global_device_ids=true, to_apply=%region_22.23 | all-reduce | flops 6144 | bytes 49152 | tf_op jit(solution)/shard_map/pmax | solution.py:68
  323.7 76.7 %psum.28 = f32[6144]{0:T(1024)S(1)} all-reduce(f32[6144]{0:T(1024)S(1)} %maximum_multiply_fusion), channel_id=1, replica_groups=mesh['row'=16,'col'=16] {'col'}, use_global_device_ids=true, to_apply=%region_23.24 | all-reduce | flops 6144 | bytes 49152 | tf_op jit(solution)/shard_map/psum | solution.py:69
  400.5 22.8 %while.98 = (s32[]{:T(128)}, f32[2048]{0:T(1024)S(1)}, f32[2048]{0:T(1024)S(1)}, f32[4,512]{1,0:T(4,128)S(1)}, f32[4,512]{1,0:T(4,128)S(1)}, /*index=5*/f32[2048...) while((s32[]{:T(128)}, f32[2048]{0:T(1024)S(1)}, ...), condition=%wide.region_41.42_spmd.clone, body=%wide.region_38.0_spmd.clone.sunk | while | flops 141568000 | bytes 8908920 | solution.py:61
  423.3 53.0 %pmax.29 = f32[6144]{0:T(1024)S(1)} all-reduce(f32[6144]{0:T(1024)S(1)} %constant_dynamic-update-slice_fusion.9), channel_id=1, replica_groups=mesh['row'=16,'col'=16] {'row'}, use_global_device_ids=true, to_apply=%region_24.25 | all-reduce | flops 6144 | bytes 49152 | tf_op jit(solution)/shard_map/pmax | solution.py:74
  476.3 53.1 %psum.29 = f32[6144]{0:T(1024)S(1)} all-reduce(f32[6144]{0:T(1024)S(1)} %maximum_multiply_fusion.1), channel_id=1, replica_groups=mesh['row'=16,'col'=16] {'row'}, use_global_device_ids=true, to_apply=%region_25.26 | all-reduce | flops 6144 | bytes 49152 | tf_op jit(solution)/shard_map/psum | solution.py:75
  529.5 26.7 %while.97 = (s32[]{:T(128)}, f32[2048]{0:T(1024)S(1)}, f32[2048]{0:T(1024)S(1)}, f32[4,512]{1,0:T(4,128)S(1)}, f32[4,512]{1,0:T(4,128)S(1)}, /*index=5*/f32[4,51...) while((s32[]{:T(128)}, f32[2048]{0:T(1024)S(1)}, ...), condition=%wide.region_31.32_spmd.clone, body=%wide.region_26.31_spmd.clone.sunk | while | flops 147858432 | bytes 8941720 | solution.py:61
  556.3 52.9 %pmax.31 = f32[4096]{0:T(1024)S(1)} all-reduce(f32[4096]{0:T(1024)S(1)} %constant_dynamic-update-slice_fusion.3), channel_id=1, replica_groups=mesh['row'=16,'col'=16] {'row'}, use_global_device_ids=true, to_apply=%region_42.43 | all-reduce | flops 4096 | bytes 32768 | tf_op jit(solution)/shard_map/pmax | solution.py:74
  609.2 52.9 %psum.31 = f32[4096]{0:T(1024)S(1)} all-reduce(f32[4096]{0:T(1024)S(1)} %maximum_multiply_fusion.3), channel_id=1, replica_groups=mesh['row'=16,'col'=16] {'row'}, use_global_device_ids=true, to_apply=%region_43.44 | all-reduce | flops 4096 | bytes 32768 | tf_op jit(solution)/shard_map/psum | solution.py:75
  662.8 7.4 while.93
  670.3 76.7 %pmax.30 = f32[4096]{0:T(1024)S(1)} all-reduce(f32[4096]{0:T(1024)S(1)} %constant_dynamic-update-slice_fusion.2), channel_id=1, replica_groups=mesh['row'=16,'col'=16] {'col'}, use_global_device_ids=true, to_apply=%region_36.37 | all-reduce | flops 4096 | bytes 32768 | tf_op jit(solution)/shard_map/pmax | solution.py:68
  747.0 76.7 %psum.30 = f32[4096]{0:T(1024)S(1)} all-reduce(f32[4096]{0:T(1024)S(1)} %maximum_multiply_fusion.2), channel_id=1, replica_groups=mesh['row'=16,'col'=16] {'col'}, use_global_device_ids=true, to_apply=%region_37.38 | all-reduce | flops 4096 | bytes 32768 | tf_op jit(solution)/shard_map/psum | solution.py:69
  (251 shorter events, 123.8 us)
Async XLA Ops:
  86.5 27.0 %copy-start = (bf16[2048,64]{0,1:T(8,128)(2,1)S(1)}, bf16[2048,64]{0,1:T(8,128)(2,1)}, u32[]{:S(2)}) copy-start(bf16[2048,64]{0,1:T(8,128)(2,1)} %param.17) | copy-start | bytes 786436
  86.6 27.1 %copy-start.1 = (bf16[2048]{0:T(1024)(128)(2,1)S(1)}, bf16[2048]{0:T(1024)(128)(2,1)}, u32[]{:S(2)}) copy-start(bf16[2048]{0:T(1024)(128)(2,1)} %param.19) | copy-start | bytes 12292
  220.2 180.3 %copy-start.2 = (bf16[2048]{0:T(1024)(128)(2,1)S(1)}, bf16[2048]{0:T(1024)(128)(2,1)}, u32[]{:S(2)}) copy-start(bf16[2048]{0:T(1024)(128)(2,1)} %param.18) | copy-start | bytes 12292
where the time goes:
time: 825 us; the launch traced here: 824 us
  blocking collectives  682 us (83%)
  other arithmetic  70.6 us (9%)
  matrix products  65.9 us (8%)
    pmax x2, blocking collectives, reduce_col(): merged_top = lax.pmax(maxima, 'col')  153 us
    psum x2, blocking collectives, reduce_col(): merged_total = lax.psum(totals * jnp.exp(maxima - merged_top), 'col')  153 us
    psum x2, blocking collectives, reduce_row(): merged_total = lax.psum(totals * jnp.exp(maxima - merged_top), 'row')  106 us
    pmax x2, blocking collectives, reduce_row(): merged_top = lax.pmax(maxima, 'row')  106 us
    dot_general x24, matrix products, advance(): lax.dot_general(piece_desc, right_desc, (((1,), (1,)), ((), ())), preferr...  65.9 us
    reduce_sum x20, other arithmetic, advance(): row_total = jnp.sum(jnp.exp(row_score - row_top[:, None]), axis=1)  56.8 us
    all_gather x1, blocking collectives, body(): source_rows = lax.all_gather(source_desc, 'col', axis=1, tiled=True)  47.2 us
    all_gather x1, blocking collectives, body(): lax.all_gather(target_mass_piece, 'col', axis=0, tiled=True)  39.8 us

commit v1 on v0

--- a/solution.py
+++ b/solution.py
@@ -8,6 +8,11 @@
 EPSILON = 0.25
 REACH = 1.0
 DAMPING = 1.0 / (1.0 + EPSILON / REACH)
+
+
+def exchange_gather(block, axis, along):
+    outgoing = jnp.stack([block] * lax.axis_size(axis))
+    return jnp.concatenate(lax.all_to_all(outgoing, axis, 0, 0), axis=along)
 
 
 def half_norms(points):
@@ -97,7 +102,7 @@
     )
     target_rows, target_row_mass = (
         lax.all_gather(target_piece, "col", axis=0, tiled=True),
-        lax.all_gather(target_mass_piece, "col", axis=0, tiled=True),
+        exchange_gather(target_mass_piece, "col", 0),
     )
     source_log = jnp.log(source_mass.astype(jnp.float32))
     source_col_log = jnp.log(source_col_mass.astype(jnp.float32))

time: 825 us -> 800 us (0.970)
  blocking collectives: 682 us -> 642 us
  starting transfers between devices: 0 us -> 10.1 us
    all_gather x1 -> x0, blocking collectives: 39.8 us -> none  [body(): lax.all_gather(target_mass_piece, 'col', axis=0, tiled=True)]
    all_to_all x0 -> x1, starting transfers between devices: none -> 10.1 us  [exchange_gather(): return jnp.concatenate(lax.all_to_all(outgoing, axis, 0, 0), axis=along)]
  transfers between devices with their start and end apart: 0 -> 1, of which waited for: 0 -> 0; matrix products, arithmetic and copies ran while one was open for 0% -> 7% of each run, Pallas kernels for 0% -> 0%
where the time goes in v1:
time: 800 us; the launch traced here: 799 us
  blocking collectives  642 us (80%)
  other arithmetic  72.2 us (9%)
  matrix products  65.9 us (8%)
  starting transfers between devices  10.1 us (1%)
    pmax x2, blocking collectives, reduce_col(): merged_top = lax.pmax(maxima, 'col')  156 us
    psum x2, blocking collectives, reduce_col(): merged_total = lax.psum(totals * jnp.exp(maxima - merged_top), 'col')  153 us
    psum x2, blocking collectives, reduce_row(): merged_total = lax.psum(totals * jnp.exp(maxima - merged_top), 'row')  106 us
    pmax x2, blocking collectives, reduce_row(): merged_top = lax.pmax(maxima, 'row')  106 us
    dot_general x24, matrix products, advance(): lax.dot_general(piece_desc, right_desc, (((1,), (1,)), ((), ())), preferr...  65.9 us
    reduce_sum x20, other arithmetic, advance(): row_total = jnp.sum(jnp.exp(row_score - row_top[:, None]), axis=1)  56.7 us
    all_gather x1, blocking collectives, body(): source_rows = lax.all_gather(source_desc, 'col', axis=1, tiled=True)  46 us
    all_gather x1, blocking collectives, body(): lax.all_gather(target_piece, 'col', axis=0, tiled=True)  39.3 us
  transfers between devices with their start and end apart: 1, of which 0 were waited for; matrix products, arithmetic and copies ran while one was open for 7% of the time, Pallas kernels for 0%

profile of v1, /device:TPU:32, one launch (start us, length us, event | category | flops | bytes accessed | tf_op | source)
XLA Modules:
  0.0 798.9 jit_solution(2023481527729715888)
XLA Ops:
  2.0 10.1 %all-to-all-start = ((bf16[16,1,128]{2,1,0:T(2,128)(2,1)}), bf16[16,1,128]{2,1,0:T(2,128)(2,1)S(1)}, u32[]{:S(2)}, u32[]{:S(2)}) async-start(bf16[16,1,128]{2,1,0:T(2,128)(2,1)} %stack.2), calls=%async_computation | async-start | bytes 16384 | tf_op jit(solution)/shard_map/all_to_all | solution.py:15
  12.1 46.0 %all-gather = bf16[16,4,2048]{2,1,0:T(4,128)(2,1)S(1)} all-gather(bf16[1,4,2048]{2,1,0:T(4,128)(2,1)} %bitcast.204), channel_id=1, replica_groups=mesh['row'=16,'col'=16] {'col'}, dimensions={0}, use_global_device_ids=true | all-gather | bytes 278528 | tf_op jit(solution)/shard_map/all_gather | solution.py:93
  58.2 19.8 %all_gather.13 = bf16[2048,64]{0,1:T(8,128)(2,1)S(1)} all-gather(bf16[128,64]{0,1:T(8,128)(2,1)S(1)} %dynamic-slice_bitcast_fusion), channel_id=1, replica_groups=mesh['row'=16,'col'=16] {'row'}, dimensions={0}, use_global_device_ids=true | all-gather | bytes 278528 | tf_op jit(solution)/shard_map/all_gather | solution.py:96
  82.4 16.1 %all-gather.1 = bf16[16,1,128]{2,1,0:T(2,128)(2,1)S(1)} all-gather(bf16[1,1,128]{2,1,0:T(2,128)(2,1)S(1)} %dynamic-slice_bitcast_fusion.1), channel_id=1, replica_groups=mesh['row'=16,'col'=16] {'row'}, dimensions={0}, use_global_device_ids=true | all-gather | bytes 4352 | tf_op jit(solution)/shard_map/all_gather | solution.py:97
  98.9 26.9 %while.95 = (s32[]{:T(128)}, f32[2048]{0:T(1024)S(1)}, f32[2048]{0:T(1024)S(1)}, f32[4,512]{1,0:T(4,128)S(1)}, f32[4,512]{1,0:T(4,128)S(1)}, /*index=5*/f32[4,51...) while((s32[]{:T(128)}, f32[2048]{0:T(1024)S(1)}, ...), condition=%wide.region_14.15_spmd.clone, body=%wide.region_9.14_spmd.clone.sunk | while | flops 147858432 | bytes 9203864 | solution.py:66
  102.1 3.4 exponential_reduce_fusion.18
  108.8 3.4 exponential_reduce_fusion.18
  115.6 3.4 exponential_reduce_fusion.18
  122.3 3.4 exponential_reduce_fusion.18
  125.9 26.7 %while.94 = (s32[]{:T(128)}, f32[2048]{0:T(1024)S(1)}, f32[2048]{0:T(1024)S(1)}, f32[4,512]{1,0:T(4,128)S(1)}, f32[4,512]{1,0:T(4,128)S(1)}, /*index=5*/f32[4,51...) while((s32[]{:T(128)}, f32[2048]{0:T(1024)S(1)}, ...), condition=%wide.region_7.8_spmd.clone, body=%wide.region_2.7_spmd.clone.sunk | while | flops 147858432 | bytes 8941720 | solution.py:66
  129.1 3.4 exponential_reduce_fusion.17
  152.6 39.3 %all_gather.15 = bf16[2048,64]{0,1:T(8,128)(2,1)S(1)} all-gather(bf16[128,64]{0,1:T(8,128)(2,1)S(1)} %constant_dynamic-slice_fusion.11), channel_id=1, replica_groups=mesh['row'=16,'col'=16] {'col'}, dimensions={0}, use_global_device_ids=true | all-gather | bytes 278528 | tf_op jit(solution)/shard_map/all_gather | solution.py:104
  192.6 26.7 %while.96 = (s32[]{:T(128)}, f32[2048]{0:T(1024)S(1)}, f32[2048]{0:T(1024)S(1)}, f32[4,512]{1,0:T(4,128)S(1)}, f32[4,512]{1,0:T(4,128)S(1)}, /*index=5*/f32[4,51...) while((s32[]{:T(128)}, f32[2048]{0:T(1024)S(1)}, ...), condition=%wide.region_21.22_spmd.clone, body=%wide.region_16.21_spmd.clone.sunk | while | flops 147858432 | bytes 8941720 | solution.py:66
  219.3 78.8 %pmax.28 = f32[6144]{0:T(1024)S(1)} all-reduce(f32[6144]{0:T(1024)S(1)} %constant_dynamic-update-slice_fusion.8), channel_id=1, replica_groups=mesh['row'=16,'col'=16] {'col'}, use_global_device_ids=true, to_apply=%region_22.23 | all-reduce | flops 6144 | bytes 49152 | tf_op jit(solution)/shard_map/pmax | solution.py:73
  298.2 76.7 %psum.28 = f32[6144]{0:T(1024)S(1)} all-reduce(f32[6144]{0:T(1024)S(1)} %maximum_multiply_fusion), channel_id=1, replica_groups=mesh['row'=16,'col'=16] {'col'}, use_global_device_ids=true, to_apply=%region_23.24 | all-reduce | flops 6144 | bytes 49152 | tf_op jit(solution)/shard_map/psum | solution.py:74
  375.0 22.8 %while.98 = (s32[]{:T(128)}, f32[2048]{0:T(1024)S(1)}, f32[2048]{0:T(1024)S(1)}, f32[4,512]{1,0:T(4,128)S(1)}, f32[4,512]{1,0:T(4,128)S(1)}, /*index=5*/f32[2048...) while((s32[]{:T(128)}, f32[2048]{0:T(1024)S(1)}, ...), condition=%wide.region_41.42_spmd.clone, body=%wide.region_38.0_spmd.clone.sunk | while | flops 141568000 | bytes 8908920 | solution.py:66
  397.8 53.0 %pmax.29 = f32[6144]{0:T(1024)S(1)} all-reduce(f32[6144]{0:T(1024)S(1)} %constant_dynamic-update-slice_fusion.9), channel_id=1, replica_groups=mesh['row'=16,'col'=16] {'row'}, use_global_device_ids=true, to_apply=%region_24.25 | all-reduce | flops 6144 | bytes 49152 | tf_op jit(solution)/shard_map/pmax | solution.py:79
  450.8 53.1 %psum.29 = f32[6144]{0:T(1024)S(1)} all-reduce(f32[6144]{0:T(1024)S(1)} %maximum_multiply_fusion.1), channel_id=1, replica_groups=mesh['row'=16,'col'=16] {'row'}, use_global_device_ids=true, to_apply=%region_25.26 | all-reduce | flops 6144 | bytes 49152 | tf_op jit(solution)/shard_map/psum | solution.py:80
  504.0 26.7 %while.97 = (s32[]{:T(128)}, f32[2048]{0:T(1024)S(1)}, f32[2048]{0:T(1024)S(1)}, f32[4,512]{1,0:T(4,128)S(1)}, f32[4,512]{1,0:T(4,128)S(1)}, /*index=5*/f32[4,51...) while((s32[]{:T(128)}, f32[2048]{0:T(1024)S(1)}, ...), condition=%wide.region_31.32_spmd.clone, body=%wide.region_26.31_spmd.clone.sunk | while | flops 147858432 | bytes 8941720 | solution.py:66
  530.7 52.9 %pmax.31 = f32[4096]{0:T(1024)S(1)} all-reduce(f32[4096]{0:T(1024)S(1)} %constant_dynamic-update-slice_fusion.3), channel_id=1, replica_groups=mesh['row'=16,'col'=16] {'row'}, use_global_device_ids=true, to_apply=%region_42.43 | all-reduce | flops 4096 | bytes 32768 | tf_op jit(solution)/shard_map/pmax | solution.py:79
  583.7 52.9 %psum.31 = f32[4096]{0:T(1024)S(1)} all-reduce(f32[4096]{0:T(1024)S(1)} %maximum_multiply_fusion.3), channel_id=1, replica_groups=mesh['row'=16,'col'=16] {'row'}, use_global_device_ids=true, to_apply=%region_43.44 | all-reduce | flops 4096 | bytes 32768 | tf_op jit(solution)/shard_map/psum | solution.py:80
  637.2 7.4 while.93
  644.7 76.8 %pmax.30 = f32[4096]{0:T(1024)S(1)} all-reduce(f32[4096]{0:T(1024)S(1)} %constant_dynamic-update-slice_fusion.2), channel_id=1, replica_groups=mesh['row'=16,'col'=16] {'col'}, use_global_device_ids=true, to_apply=%region_36.37 | all-reduce | flops 4096 | bytes 32768 | tf_op jit(solution)/shard_map/pmax | solution.py:73
  721.5 76.7 %psum.30 = f32[4096]{0:T(1024)S(1)} all-reduce(f32[4096]{0:T(1024)S(1)} %maximum_multiply_fusion.2), channel_id=1, replica_groups=mesh['row'=16,'col'=16] {'col'}, use_global_device_ids=true, to_apply=%region_37.38 | all-reduce | flops 4096 | bytes 32768 | tf_op jit(solution)/shard_map/psum | solution.py:74
  (254 shorter events, 127.4 us)
Async XLA Ops:
  2.0 190.5 %all-to-all-start = ((bf16[16,1,128]{2,1,0:T(2,128)(2,1)}), bf16[16,1,128]{2,1,0:T(2,128)(2,1)S(1)}, u32[]{:S(2)}, u32[]{:S(2)}) async-start(bf16[16,1,128]{2,1,0:T(2,128)(2,1)} %stack.2), calls=%async_computation | async-start | bytes 16384 | tf_op jit(solution)/shard_map/all_to_all | solution.py:15
  98.9 27.0 %copy-start = (bf16[2048,64]{0,1:T(8,128)(2,1)S(1)}, bf16[2048,64]{0,1:T(8,128)(2,1)}, u32[]{:S(2)}) copy-start(bf16[2048,64]{0,1:T(8,128)(2,1)} %param.17) | copy-start | bytes 786436
  192.6 182.4 %copy-start.1 = (bf16[2048]{0:T(1024)(128)(2,1)S(1)}, bf16[2048]{0:T(1024)(128)(2,1)}, u32[]{:S(2)}) copy-start(bf16[2048]{0:T(1024)(128)(2,1)} %param.18) | copy-start | bytes 12292
  375.0 128.9 %copy-start.2 = (bf16[2048]{0:T(1024)(128)(2,1)S(1)}, bf16[2048]{0:T(1024)(128)(2,1)}, u32[]{:S(2)}) copy-start(bf16[2048]{0:T(1024)(128)(2,1)} %param.19) | copy-start | bytes 12292
